TPU v7x, 512 devices: a whole 4x8x8 slice. The times are simulated.
512 devices in a mesh: wide: 32 (over y, x), narrow: 16 (over z, core).
Axes of the slice: x: 4, y: 8, z: 8, core: 2. Of those that a mesh axis runs over, the one named last changes fastest.
Arguments:
- hamiltonian: float32 [1024, 3, 128, 128], P(('wide', 'narrow')), may hold values from -3.3 to 3.3, as said below
- old_density: float32 [1024, 3, 128, 128], P(('wide', 'narrow')), may hold values from -2 to 2
- neighbours: int32 [1024, 3], P(('wide', 'narrow')), may hold values from 0 to 31, as said below
- live: int32 [1024], P(('wide', 'narrow')), may hold values from 0 to 1, as said below
- potential: float32 [1], replicated, may hold values from -1 to 1
Outputs:
- density: float32 [1024, 3, 128, 128], P(('wide', 'narrow'))
Inputs may be any that keep to these rules, and one draw needn't show every extreme that they name: Within each cluster of 32 consecutive blocks, entry 0 is the block's own index in the cluster and entries 1 and 2 are its neighbours on a cycle through all blocks of the cluster: block a is entry 1 of its entry-2 neighbour and entry 2 of its entry-1 neighbour. Along the cycle the 2 blocks of one device stand next to each other in some order; the devices of the narrow axis follow each other in an order drawn from the seed. For each index of the narrow axis, the devices at wide indices i and i + 16 own at most 2 live blocks together; in every draw some device owns 2 live blocks. `hamiltonian`: the block Hamiltonian is symmetric: tile 1 of block c is the transpose of tile 2 of prev(c), and tile 0 is symmetric.
All inputs are finite; a program needn't handle non-finite values. Where the computation divides by a largest or mean magnitude, that divisor is 1e-20 or more.
Results may differ from a plain program's by a relative error of at most 0.0001.
Values sent between devices are 32-bit elements; how exact they have to be, the bound alone decides.
A program may use at most 64 MiB of HBM per device.

v0:
```python
import jax
import jax.numpy as jnp
from jax import lax
from jax.sharding import PartitionSpec as P

ITERS = 4
epsilon = 1e-06


def in_one_piece(arrays, axis, dim, along):
    widths = [a.shape[along] for a in arrays]
    both = jnp.concatenate(arrays, axis=along)
    out = lax.all_gather(both, axis, axis=dim, tiled=True)
    return tuple(jnp.split(out, [sum(widths[:k]) for k in range(1, len(widths))], axis=along))


def product(left, right):
    return jnp.matmul(left, right, precision=lax.Precision.HIGHEST)


def transpose_tiles(tiles):
    return jnp.swapaxes(tiles, -1, -2)


def assemble(row_tiles, prev_onsite, next_onsite, level):
    zero_tile = jnp.zeros_like(prev_onsite)
    upper_rows = jnp.concatenate(
        [row_tiles[..., 0, :, :], row_tiles[..., 1, :, :], row_tiles[..., 2, :, :]], axis=-1
    )
    middle_rows = jnp.concatenate(
        [transpose_tiles(row_tiles[..., 1, :, :]), prev_onsite, zero_tile], axis=-1
    )
    lower_rows = jnp.concatenate(
        [transpose_tiles(row_tiles[..., 2, :, :]), zero_tile, next_onsite], axis=-1
    )
    matrix = jnp.concatenate([upper_rows, middle_rows, lower_rows], axis=-2)
    order = matrix.shape[-1]
    return matrix - level * jnp.eye(order, dtype=jnp.float32)


def sign_columns(matrix, width, depth):
    order = matrix.shape[-1]
    identity = jnp.eye(order, dtype=jnp.float32)
    bound = jnp.max(jnp.sum(jnp.abs(matrix), axis=-1), axis=-1) + epsilon
    current = matrix / bound[..., None, None]
    for sweep in range(depth - 1):
        square = product(current, current)
        current = 0.5 * product(current, 3.0 * identity - square)
    square = product(current, current)
    final_cols = 0.5 * product(current, 3.0 * identity[:, :width] - square[..., :, :width])
    columns = 0.5 * (identity[:, :width] - final_cols)
    return columns.reshape(columns.shape[:-2] + (order // width, width, width))


def shards(hamiltonian, old_density, neighbours, live, potential):
    width = hamiltonian.shape[-1]
    level = potential[0]
    cluster_onsite = lax.all_gather(hamiltonian[:, 0], "narrow", axis=0, tiled=True)
    prev_onsite = jnp.take(cluster_onsite, neighbours[:, 1], axis=0)
    next_onsite = jnp.take(cluster_onsite, neighbours[:, 2], axis=0)
    matrices = assemble(hamiltonian, prev_onsite, next_onsite, level)
    new_cols = sign_columns(matrices, width, ITERS)
    fresh_cols = jnp.where(live[:, None, None, None] == 1, new_cols, old_density)
    prev_side, next_side = in_one_piece((fresh_cols[:, 1], fresh_cols[:, 2]), "narrow", 0, 1)
    from_prev = jnp.take(next_side, neighbours[:, 1], axis=0)
    from_next = jnp.take(prev_side, neighbours[:, 2], axis=0)
    return jnp.stack(
        [
            0.5 * (fresh_cols[:, 0] + transpose_tiles(fresh_cols[:, 0])),
            0.5 * (fresh_cols[:, 1] + transpose_tiles(from_prev)),
            0.5 * (fresh_cols[:, 2] + transpose_tiles(from_next)),
        ],
        axis=1,
    )


def solution(mesh):
    placed = (
        P(("wide", "narrow"), None, None, None),
        P(("wide", "narrow"), None, None, None),
        P(("wide", "narrow"), None),
        P(("wide", "narrow")),
        P(),
    )
    return jax.shard_map(
        shards,
        mesh=mesh,
        in_specs=placed,
        out_specs=P(("wide", "narrow"), None, None, None),
        check_vma=False,
    )
```

profile of v0, /device:TPU:1, one launch (start us, length us, event | category | flops | bytes accessed | tf_op | source)
XLA Modules:
  0.0 140.7 jit_solution(15930580519983071181)
XLA Ops:
  6.5 1.8 %slice_bitcast_fusion.5 = (f32[2,128,128]{2,1,0:T(8,128)S(1)}, f32[2,128,128]{2,1,0:T(8,128)S(1)}, f32[2,128,128]{2,1,0:T(8,128)S(1)}, f32[2,1,128,128]{3,2,1,0:...) fusion(f32[2,3,128,128]{3,2,1,0:T(8,128)} %param.7), kind=kLoop, calls=%fused_computation.51 | loop fusion | bytes 1179648 | tf_op jit(solution)/shard_map/squeeze | solution.py:28
  9.0 0.1 copy.68
  9.2 0.2 slice_reduce_fusion.1
  9.7 48.9 %all-gather.6.cloned.1.call-done = f32[32,1,128,128]{3,2,1,0:T(8,128)} async-done(((f32[2,1,128,128]{3,2,1,0:T(8,128)}), f32[32,1,128,128]{3,2,1,0:T(8,128)}) %all-gather.6.cloned.1.call-update) | async-done | bytes 2097168 | tf_op jit(solution)/shard_map/all_gather | solution.py:58
  58.6 2.1 %gather_fusion.1 = f32[2,128,128]{2,1,0:T(8,128)S(1)} fusion(f32[32,128,128]{2,1,0:T(8,128)} %bitcast.68, s32[1024]{0:T(1024)S(1)} %pad_clamp_fusion), kind=kCustom, calls=%fused_computation.1.clone | custom fusion | bytes 262152 | tf_op jit(solution)/shard_map/jit(_take)/gather | solution.py:60
  60.8 2.1 %gather_fusion = f32[2,128,128]{2,1,0:T(8,128)S(1)} fusion(f32[32,128,128]{2,1,0:T(8,128)} %bitcast.69, s32[1024]{0:T(1024)S(1)} %pad_clamp_fusion.1), kind=kCustom, calls=%fused_computation.clone | custom fusion | bytes 262152 | tf_op jit(solution)/shard_map/jit(_take)/gather | solution.py:59
  63.1 0.2 abs_reduce_fusion
  63.3 0.1 reduce_max.9
  63.5 2.6 %convolution_subtract_fusion.2 = f32[2,384,384]{2,1,0:T(8,128)S(1)} fusion(f32[384,384]{1,0:T(8,128)S(1)} %fusion.3, f32[2]{0:T(128)S(1)} %broadcast_add_fusion, f32[2,128,128]{2,1,0:T(8,128)S(1)} %broadcast_select_fusion, f32[2,128,128]{2,1,0:T(8,128)S(1)} %broadcast_in_dim.17, f32[2,128,128]{2,1,0:T(8,128)S(1)} %bitcast.66, ...), kind=kOutput, calls=%fused_computation.9 | convolution fusion | flops 1362198528 | bytes 3407880 | tf_op jit(solution)/shard_map/dot_general | solution.py:18
  66.1 2.5 %convolution_multiply_fusion.2 = f32[2,384,384]{2,1,0:T(8,128)S(1)} fusion(f32[2,384,384]{2,1,0:T(8,128)S(1)} %convolution_subtract_fusion.2, f32[2]{0:T(128)S(1)} %broadcast_add_fusion, f32[2,128,128]{2,1,0:T(8,128)S(1)} %broadcast_select_fusion, f32[2,128,128]{2,1,0:T(8,128)S(1)} %broadcast_in_dim.17, f32[2,128,128]{2,1,0:T(8,128)S(1)} %bitcast.67, ...), kind=kOutput, calls=%fused_computation.8 | convolution fusion | flops 1362198528 | bytes 3997704 | tf_op jit(solution)/shard_map/dot_general | solution.py:18
  68.6 2.5 %convolution_subtract_fusion.1 = f32[2,384,384]{2,1,0:T(8,128)S(1)} fusion(f32[2,384,384]{2,1,0:T(8,128)S(1)} %convolution_multiply_fusion.2, f32[384,384]{1,0:T(8,128)S(1)} %fusion.3), kind=kOutput, calls=%fused_computation.7 | convolution fusion | flops 1359249408 | bytes 2949120 | tf_op jit(solution)/shard_map/dot_general | solution.py:18
  71.1 2.4 %convolution_multiply_fusion.1 = f32[2,384,384]{2,1,0:T(8,128)S(1)} fusion(f32[2,384,384]{2,1,0:T(8,128)S(1)} %convolution_multiply_fusion.2, f32[2,384,384]{2,1,0:T(8,128)S(1)} %convolution_subtract_fusion.1), kind=kOutput, calls=%fused_computation.6 | convolution fusion | flops 1359249408 | bytes 3538944 | tf_op jit(solution)/shard_map/dot_general | solution.py:18
  73.5 2.7 %convolution_subtract_fusion = f32[2,384,384]{2,1,0:T(8,128)S(1)} fusion(f32[2,384,384]{2,1,0:T(8,128)S(1)} %convolution_multiply_fusion.1, f32[384,384]{1,0:T(8,128)S(1)} %fusion.3), kind=kOutput, calls=%fused_computation.5 | convolution fusion | flops 1359249408 | bytes 2949120 | tf_op jit(solution)/shard_map/dot_general | solution.py:18
  76.2 2.4 %convolution_multiply_fusion = f32[2,384,384]{2,1,0:T(8,128)S(1)} fusion(f32[2,384,384]{2,1,0:T(8,128)S(1)} %convolution_multiply_fusion.1, f32[2,384,384]{2,1,0:T(8,128)S(1)} %convolution_subtract_fusion), kind=kOutput, calls=%fused_computation.4 | convolution fusion | flops 1359249408 | bytes 3538944 | tf_op jit(solution)/shard_map/dot_general | solution.py:18
  78.7 1.2 convolution_subtract_fusion.3
  79.9 1.2 fusion.1
  81.1 0.1 copy_select_fusion
  81.2 0.7 pad_maximum_fusion.1
  81.9 0.1 copy.63
  82.2 43.7 %all-gather.4.cloned.1.call-done = f32[32,256,128]{2,1,0:T(8,128)} async-done(((f32[2,256,128]{2,1,0:T(8,128)}), f32[32,256,128]{2,1,0:T(8,128)}) %all-gather.4.cloned.1.call-update) | async-done | bytes 4194320 | tf_op jit(solution)/shard_map/all_gather | solution.py:13
  125.9 3.9 %fusion.9 = (f32[32,128,128]{2,1,0:T(8,128)}, f32[32,128,128]{2,1,0:T(8,128)S(1)}) fusion(f32[32,256,128]{2,1,0:T(8,128)} %all-gather.4.cloned.1.call-done), kind=kLoop, calls=%fused_computation.52 | loop fusion | bytes 8388608 | tf_op jit(solution)/shard_map/split | solution.py:14
  129.8 2.1 %gather_fusion.2 = f32[2,128,128]{2,1,0:T(8,128)S(1)} fusion(f32[32,128,128]{2,1,0:T(8,128)} %get-tuple-element.8, s32[1024]{0:T(1024)S(1)} %pad_clamp_fusion.1), kind=kCustom, calls=%fused_computation.2.clone | custom fusion | bytes 262152 | tf_op jit(solution)/shard_map/jit(_take)/gather | solution.py:65
  131.9 0.6 gather_fusion.3
  132.9 0.9 copy.66
  (34 shorter events, 1.1 us)
Async XLA Ops:
  6.5 2.7 %copy-start.1 = (s32[2,3]{1,0:T(2,128)S(1)}, s32[2,3]{1,0:T(2,128)}, u32[]{:S(2)}) copy-start(s32[2,3]{1,0:T(2,128)} %param.9) | copy-start | bytes 76
  6.5 52.1 %all-gather.6.cloned.1.call-start = ((), (), s32[]{:S(2)}) async-start(), calls=%async_computation.1 | async-start | bytes 2228224 | tf_op jit(solution)/shard_map/all_gather | solution.py:58
  8.3 1.3 copy-start.2
  8.3 117.5 %all-gather.4.cloned.1.call-start = ((), (), s32[]{:S(2)}) async-start(), calls=%async_computation | async-start | bytes 4456448 | tf_op jit(solution)/shard_map/all_gather | solution.py:13
  79.8 1.2 copy-start
Sparse Core Ops, SparseCore 0:
  9.5 49.0 all-gather.5
  82.1 43.7 all-gather.3
where the time goes:
time: 141 us
  waiting for transfers between devices  92.6 us (66%)
  matrix products  17.5 us (12%)
  local copies, waits for them, and re-layouts  14.4 us (10%)
  between operations  14.3 us (10%)
  other arithmetic  1.79 us (1%)
    all_gather x1, waiting for transfers between devices, shards(): lax.all_gather(hamiltonian[:, 0], 'narrow', axis=0, tiled=True)  48.9 us
    all_gather x1, waiting for transfers between devices, in_one_piece(): out = lax.all_gather(both, axis, axis=dim, tiled=True)  43.7 us
    dot_general x8, matrix products, product(): return jnp.matmul(left, right, precision=lax.Precision.HIGHEST)  17.5 us
    split x1, local copies, waits for them, and re-layouts, in_one_piece(): jnp.split(out, [sum(widths[:k]) for k in range(1, len(widths))], axis=along)  3.92 us
  transfers between devices with their start and end apart: 2, of which 2 were waited for; matrix products, arithmetic and copies ran while one was open for 1% of the time, Pallas kernels for 0%

commit v1 on v0

--- a/solution.py
+++ b/solution.py
@@ -5,6 +5,11 @@
 
 ITERS = 4
 epsilon = 1e-06
+
+
+def swapped_in(block, name, dim):
+    sent = jnp.stack([block] * lax.axis_size(name))
+    return jnp.concatenate(lax.all_to_all(sent, name, 0, 0), axis=dim)
 
 
 def in_one_piece(arrays, axis, dim, along):
@@ -55,7 +60,7 @@
 def shards(hamiltonian, old_density, neighbours, live, potential):
     width = hamiltonian.shape[-1]
     level = potential[0]
-    cluster_onsite = lax.all_gather(hamiltonian[:, 0], "narrow", axis=0, tiled=True)
+    cluster_onsite = swapped_in(hamiltonian[:, 0], "narrow", 0)
     prev_onsite = jnp.take(cluster_onsite, neighbours[:, 1], axis=0)
     next_onsite = jnp.take(cluster_onsite, neighbours[:, 2], axis=0)
     matrices = assemble(hamiltonian, prev_onsite, next_onsite, level)

time: 141 us -> 154 us (1.092)
  starting transfers between devices: 0.04 us -> 12 us
  other arithmetic: 1.79 us -> 5.66 us
  waiting for transfers between devices: 92.6 us -> 89.1 us
    all_gather x1 -> x0, waiting for transfers between devices: 48.9 us -> none  [shards(): lax.all_gather(hamiltonian[:, 0], 'narrow', axis=0, tiled=True)]
    all_to_all x0 -> x1, waiting for transfers between devices: none -> 44.5 us  [swapped_in(): return jnp.concatenate(lax.all_to_all(sent, name, 0, 0), axis=dim)]
    all_to_all x0 -> x1, starting transfers between devices: none -> 12 us  [swapped_in(): return jnp.concatenate(lax.all_to_all(sent, name, 0, 0), axis=dim)]
    gather x1, local copies, waits for them, and re-layouts: 2.14 us -> 0.56 us  [shards(): next_onsite = jnp.take(cluster_onsite, neighbours[:, 2], axis=0)]
    another operation x0 -> x1, local copies, waits for them, and re-layouts: none -> 1.58 us  [swapped_in(): sent = jnp.stack([block] * lax.axis_size(name))]
  transfers between devices with their start and end apart: 2 -> 2, of which waited for: 2 -> 2; matrix products, arithmetic and copies ran while one was open for 1% -> 3% of each run, Pallas kernels for 0% -> 0%
where the time goes in v1:
time: 154 us; the launch traced here: 153 us
  waiting for transfers between devices  89.1 us (58%)
  matrix products  17.4 us (11%)
  local copies, waits for them, and re-layouts  14.8 us (10%)
  between operations  14.4 us (9%)
  starting transfers between devices  12 us (8%)
  other arithmetic  5.66 us (4%)
    all_gather x1, waiting for transfers between devices, in_one_piece(): out = lax.all_gather(both, axis, axis=dim, tiled=True)  44.7 us
    all_to_all x1, waiting for transfers between devices, swapped_in(): return jnp.concatenate(lax.all_to_all(sent, name, 0, 0), axis=dim)  44.5 us
    dot_general x8, matrix products, product(): return jnp.matmul(left, right, precision=lax.Precision.HIGHEST)  17.4 us
    all_to_all x1, starting transfers between devices, swapped_in(): return jnp.concatenate(lax.all_to_all(sent, name, 0, 0), axis=dim)  12 us
    split x1, local copies, waits for them, and re-layouts, in_one_piece(): jnp.split(out, [sum(widths[:k]) for k in range(1, len(widths))], axis=along)  3.93 us
  transfers between devices with their start and end apart: 2, of which 2 were waited for; matrix products, arithmetic and copies ran while one was open for 3% of the time, Pallas kernels for 0%

profile of v1, /device:TPU:1, one launch (start us, length us, event | category | flops | bytes accessed | tf_op | source)
XLA Modules:
  0.0 153.4 jit_solution(16390120345698410963)
XLA Ops:
  6.5 1.8 %slice_bitcast_fusion.5 = (f32[2,128,128]{2,1,0:T(8,128)}, f32[2,128,128]{2,1,0:T(8,128)}, f32[2,1,128,128]{3,2,1,0:T(8,128)S(1)}, f32[2,128,128]{2,1,0:T(8,128)S(1)}, f32[2,1,128,128]{3,2,1,0:T(8,128)S(1)}) fusion(f32[2,3,128,128]{3,2,1,0:T(8,128)} %param.7), kind=kLoop, calls=%fused_computation.51 | loop fusion | bytes 1048576 | tf_op jit(solution)/shard_map/squeeze | solution.py:33
  8.3 1.6 %stack.15 = f32[16,2,128,128]{3,2,1,0:T(8,128)} broadcast(f32[2,128,128]{2,1,0:T(8,128)S(1)} %get-tuple-element.16), dimensions={1,2,3} | broadcast | bytes 2228224 | tf_op jit(solution)/shard_map/stack | solution.py:11
  9.9 12.0 %all-to-all-start = ((f32[16,2,128,128]{3,2,1,0:T(8,128)}), f32[16,2,128,128]{3,2,1,0:T(8,128)S(1)}, u32[]{:S(2)}, u32[]{:S(2)}) async-start(f32[16,2,128,128]{3,2,1,0:T(8,128)} %stack.15), calls=%async_computation | async-start | bytes 4194304 | tf_op jit(solution)/shard_map/all_to_all | solution.py:12
  22.6 0.7 copy.62
  23.3 0.7 copy.63
  25.0 0.7 slice_select_fusion
  25.7 0.7 slice_convert_fusion
  26.3 44.5 %all-to-all-done = f32[16,2,128,128]{3,2,1,0:T(8,128)S(1)} async-done(((f32[16,2,128,128]{3,2,1,0:T(8,128)}), f32[16,2,128,128]{3,2,1,0:T(8,128)S(1)}, u32[]{:S(2)}, u32[]{:S(2)}) %all-to-all-start) | async-done | bytes 2097184 | tf_op jit(solution)/shard_map/all_to_all | solution.py:12
  71.4 1.2 gather_fusion
  72.6 1.0 broadcast_select_fusion.1
  73.7 1.3 abs_reduce_fusion
  75.2 2.6 %convolution_subtract_fusion.2 = f32[2,384,384]{2,1,0:T(8,128)S(1)} fusion(f32[384,384]{1,0:T(8,128)S(1)} %fusion.3, f32[2]{0:T(128)S(1)} %broadcast_add_fusion, f32[2,128,128]{2,1,0:T(8,128)S(1)} %broadcast_select_fusion, f32[2,128,128]{2,1,0:T(8,128)S(1)} %broadcast_in_dim.17, f32[2,128,128]{2,1,0:T(8,128)S(1)} %bitcast.64, ...), kind=kOutput, calls=%fused_computation.9 | convolution fusion | flops 1362198528 | bytes 3407880 | tf_op jit(solution)/shard_map/dot_general | solution.py:23
  77.9 2.4 %convolution_multiply_fusion.2 = f32[2,384,384]{2,1,0:T(8,128)S(1)} fusion(f32[2,384,384]{2,1,0:T(8,128)S(1)} %convolution_subtract_fusion.2, f32[2]{0:T(128)S(1)} %broadcast_add_fusion, f32[2,128,128]{2,1,0:T(8,128)S(1)} %broadcast_select_fusion, f32[2,128,128]{2,1,0:T(8,128)S(1)} %broadcast_in_dim.17, f32[2,128,128]{2,1,0:T(8,128)S(1)} %bitcast.65, ...), kind=kOutput, calls=%fused_computation.8 | convolution fusion | flops 1362198528 | bytes 3997704 | tf_op jit(solution)/shard_map/dot_general | solution.py:23
  80.3 2.5 %convolution_subtract_fusion.1 = f32[2,384,384]{2,1,0:T(8,128)S(1)} fusion(f32[2,384,384]{2,1,0:T(8,128)S(1)} %convolution_multiply_fusion.2, f32[384,384]{1,0:T(8,128)S(1)} %fusion.3), kind=kOutput, calls=%fused_computation.7 | convolution fusion | flops 1359249408 | bytes 2949120 | tf_op jit(solution)/shard_map/dot_general | solution.py:23
  82.8 2.4 %convolution_multiply_fusion.1 = f32[2,384,384]{2,1,0:T(8,128)S(1)} fusion(f32[2,384,384]{2,1,0:T(8,128)S(1)} %convolution_multiply_fusion.2, f32[2,384,384]{2,1,0:T(8,128)S(1)} %convolution_subtract_fusion.1), kind=kOutput, calls=%fused_computation.6 | convolution fusion | flops 1359249408 | bytes 3538944 | tf_op jit(solution)/shard_map/dot_general | solution.py:23
  85.2 2.7 %convolution_subtract_fusion = f32[2,384,384]{2,1,0:T(8,128)S(1)} fusion(f32[2,384,384]{2,1,0:T(8,128)S(1)} %convolution_multiply_fusion.1, f32[384,384]{1,0:T(8,128)S(1)} %fusion.3), kind=kOutput, calls=%fused_computation.5 | convolution fusion | flops 1359249408 | bytes 2949120 | tf_op jit(solution)/shard_map/dot_general | solution.py:23
  87.9 2.4 %convolution_multiply_fusion = f32[2,384,384]{2,1,0:T(8,128)S(1)} fusion(f32[2,384,384]{2,1,0:T(8,128)S(1)} %convolution_multiply_fusion.1, f32[2,384,384]{2,1,0:T(8,128)S(1)} %convolution_subtract_fusion), kind=kOutput, calls=%fused_computation.4 | convolution fusion | flops 1359249408 | bytes 3538944 | tf_op jit(solution)/shard_map/dot_general | solution.py:23
  90.4 1.2 convolution_subtract_fusion.3
  91.6 1.2 fusion.1
  93.0 0.7 pad_maximum_fusion.1
  93.9 44.7 %all-gather.2.cloned.1.call-done = f32[32,256,128]{2,1,0:T(8,128)} async-done(((f32[2,256,128]{2,1,0:T(8,128)}), f32[32,256,128]{2,1,0:T(8,128)}) %all-gather.2.cloned.1.call-update) | async-done | bytes 4194320 | tf_op jit(solution)/shard_map/all_gather | solution.py:18
  138.6 3.9 %fusion.9 = (f32[32,128,128]{2,1,0:T(8,128)}, f32[32,128,128]{2,1,0:T(8,128)S(1)}) fusion(f32[32,256,128]{2,1,0:T(8,128)} %all-gather.2.cloned.1.call-done), kind=kLoop, calls=%fused_computation.52 | loop fusion | bytes 8388608 | tf_op jit(solution)/shard_map/split | solution.py:19
  142.5 2.1 %gather_fusion.2 = f32[2,128,128]{2,1,0:T(8,128)S(1)} fusion(f32[32,128,128]{2,1,0:T(8,128)} %get-tuple-element.8, s32[1024]{0:T(1024)S(1)} %pad_clamp_fusion.1), kind=kCustom, calls=%fused_computation.2.clone | custom fusion | bytes 262152 | tf_op jit(solution)/shard_map/jit(_take)/gather | solution.py:70
  145.7 0.9 copy.61
  (48 shorter events, 3.0 us)
Async XLA Ops:
  9.9 14.2 %copy-start.7 = (s32[2,3]{1,0:T(2,128)S(1)}, s32[2,3]{1,0:T(2,128)}, u32[]{:S(2)}) copy-start(s32[2,3]{1,0:T(2,128)} %param.9) | copy-start | bytes 76
  9.9 60.9 %all-to-all-start = ((f32[16,2,128,128]{3,2,1,0:T(8,128)}), f32[16,2,128,128]{3,2,1,0:T(8,128)S(1)}, u32[]{:S(2)}, u32[]{:S(2)}) async-start(f32[16,2,128,128]{3,2,1,0:T(8,128)} %stack.15), calls=%async_computation | async-start | bytes 4194304 | tf_op jit(solution)/shard_map/all_to_all | solution.py:12
  21.9 2.6 %copy-start.9 = (s32[2]{0:T(128)S(1)}, s32[2]{0:T(128)}, u32[]{:S(2)}) copy-start(s32[2]{0:T(128)} %param.10) | copy-start | bytes 28
  21.9 116.7 %all-gather.2.cloned.1.call-start = ((), (), s32[]{:S(2)}) async-start(), calls=%async_computation.1 | async-start | bytes 4456448 | tf_op jit(solution)/shard_map/all_gather | solution.py:18
  72.6 2.6 %copy-start.2 = (f32[2,1,128,128]{2,3,0,1:T(8,128)S(1)}, f32[2,1,128,128]{2,3,0,1:T(8,128)}, u32[]{:S(2)}) copy-start(f32[2,1,128,128]{2,3,0,1:T(8,128)} %copy.62) | copy-start | bytes 393220
  72.6 2.6 %copy-start.3 = (f32[2,1,128,128]{2,3,0,1:T(8,128)S(1)}, f32[2,1,128,128]{2,3,0,1:T(8,128)}, u32[]{:S(2)}) copy-start(f32[2,1,128,128]{2,3,0,1:T(8,128)} %copy.63) | copy-start | bytes 393220
  72.6 2.6 %copy-start.4 = (f32[2,128,128]{2,1,0:T(8,128)S(1)}, f32[2,128,128]{2,1,0:T(8,128)}, u32[]{:S(2)}) copy-start(f32[2,128,128]{2,1,0:T(8,128)} %get-tuple-element.13) | copy-start | bytes 393220
  72.6 2.6 %copy-start.5 = (f32[2,128,128]{2,1,0:T(8,128)S(1)}, f32[2,128,128]{2,1,0:T(8,128)}, u32[]{:S(2)}) copy-start(f32[2,128,128]{2,1,0:T(8,128)} %get-tuple-element.14) | copy-start | bytes 393220
  87.9 2.5 %copy-start.1 = (f32[384,128]{1,0:T(8,128)S(1)}, f32[384,128]{1,0:T(8,128)}, u32[]{:S(2)}) copy-start(f32[384,128]{1,0:T(8,128)} %slice_select_fusion) | copy-start | bytes 589828
  90.4 1.2 copy-start
  91.6 1.2 copy-start.6
  91.6 1.2 copy-start.8
Sparse Core Ops, SparseCore 0:
  93.8 44.7 all-gather.1
